TPU v7x, 256 devices: a whole 4x4x8 slice. The times are simulated.
256 devices in a mesh: seq: 32 (over z, x), head: 8 (over y, core).
Axes of the slice: x: 4, y: 4, z: 8, core: 2. Of those that a mesh axis runs over, the one named last changes fastest.
Arguments:
- tokens: bfloat16 [32768, 1024], P(('seq', 'head')), may hold values from -6 to 6
- win_first: int32 [32768], P('seq'), may hold values from 0 to 32767, as said below
- win_count: int32 [32768], P('seq'), may hold values from 1 to 64, as said below
- norm1_gain: float32 [1024], replicated, may hold values from 0.25 to 1.75
- qkv_weight: bfloat16 [1024, 3, 1024], P('seq', None, 'head'), may hold values from -0.1875 to 0.1875
- qk_gain: float32 [2, 16, 64], P(None, 'head'), may hold values from 0.25 to 1.75
- out_weight: bfloat16 [1024, 1024], P('head', 'seq'), may hold values from -0.1875 to 0.1875
- norm2_gain: float32 [1024], replicated, may hold values from 0.25 to 1.75
- up_weight: bfloat16 [1024, 4096], P('seq', 'head'), may hold values from -0.1875 to 0.1875
- down_weight: bfloat16 [4096, 1024], P('head', 'seq'), may hold values from -0.09375 to 0.09375
Outputs:
- block_out: bfloat16 [32768, 1024], P(('seq', 'head'))
Inputs may be any that keep to these rules, and one draw needn't show every extreme that they name: Each token's window block is the run of consecutive tokens from win_first to win_first + win_count - 1, which contains the token; window blocks tile the tokens in order, and some window block has exactly 64 tokens. `win_count`: all tokens of one window block carry the same count.
All inputs are finite; a program needn't handle non-finite values.
Results may differ from a plain program's by a relative error of at most 0.008.
Values may be sent and summed in bfloat16 or wider, within the bound.
No kernel may reach another device: no remote copies, remote signals or barrier semaphores. Data moves between devices by JAX's collectives and lax.ppermute only.
A program may use at most 64 MiB of HBM per device.

v0:
```python
import math
import jax
import jax.numpy as jnp
from jax import lax
from jax.sharding import PartitionSpec as P

WIN_MOST = 64


def extended(value, sides, width):
    for axis, dim in sides:
        peers, length = (lax.axis_size(axis), value.shape[dim])
        up = [(i, (i + 1) % peers) for i in range(peers - 1)]
        down = [(j, i) for i, j in up]
        last = lax.slice_in_dim(value, length - width, length, axis=dim)
        leading = lax.slice_in_dim(value, 0, width, axis=dim)
        before = lax.ppermute(last, axis, up)
        after = lax.ppermute(leading, axis, down)
        value = jnp.concatenate([before, value, after], axis=dim)
    return value


def layer_norm(rows, gain):
    values = rows.astype(jnp.float32)
    center = values - jnp.mean(values, axis=-1, keepdims=True)
    spread = jnp.mean(center * center, axis=-1, keepdims=True)
    return (center * lax.rsqrt(spread + 1e-06) * gain).astype(jnp.bfloat16)


def head_norm(values, gain):
    scale = lax.rsqrt(jnp.mean(values * values, axis=-1, keepdims=True) + 1e-06)
    return (values * scale * gain).astype(jnp.bfloat16)


def local(
    tokens,
    win_first,
    win_count,
    norm1_gain,
    qkv_weight,
    qk_gain,
    out_weight,
    norm2_gain,
    up_weight,
    down_weight,
):
    tok_rows, model_width = tokens.shape
    head_group = lax.axis_size("head")
    seq_rows = tok_rows * head_group
    local_heads = qk_gain.shape[1]
    head_width = qk_gain.shape[2]
    columns = local_heads * head_width
    normed_one = layer_norm(tokens, norm1_gain)
    qkv_full = lax.all_gather(qkv_weight, "seq", axis=0, tiled=True).reshape(
        model_width, 3 * columns
    )
    piece = lax.all_gather(normed_one, "head", axis=0, tiled=True)
    qkv = jnp.dot(piece, qkv_full, preferred_element_type=jnp.float32).reshape(
        piece.shape[0], 3, columns
    )
    queries = head_norm(qkv[:, 0].reshape(seq_rows, local_heads, head_width), qk_gain[0])
    keys = head_norm(qkv[:, 1].reshape(seq_rows, local_heads, head_width), qk_gain[1])
    values = qkv[:, 2].astype(jnp.bfloat16)
    stacked = jnp.stack([keys.reshape(seq_rows, columns), values], axis=1)
    padded = extended(stacked, (("seq", 0),), WIN_MOST)
    row_block = math.gcd(512, seq_rows)
    key_span = row_block + 2 * WIN_MOST
    scale = head_width ** (-0.5)
    anchor = lax.axis_index("seq") * seq_rows
    outputs = []
    for first_row in range(0, seq_rows, row_block):
        query_part = queries[first_row : first_row + row_block]
        key_block = padded[first_row : first_row + key_span]
        key_part = key_block[:, 0].reshape(key_span, local_heads, head_width)
        value_part = key_block[:, 1].reshape(key_span, local_heads, head_width)
        scores = (
            jnp.einsum("qhd,khd->hqk", query_part, key_part, preferred_element_type=jnp.float32)
            * scale
        )
        lower = win_first[first_row : first_row + row_block]
        upper = lower + win_count[first_row : first_row + row_block]
        key_index = anchor + (first_row - WIN_MOST) + jnp.arange(key_span, dtype=jnp.int32)
        allowed = (key_index[None, :] >= lower[:, None]) & (key_index[None, :] < upper[:, None])
        weights = jnp.where(allowed[None], jnp.exp(scores), jnp.float32(0.0))
        total = jnp.sum(weights, axis=-1, keepdims=True)
        probs = (weights / total).astype(jnp.bfloat16)
        mixed = jnp.einsum("hqk,khd->qhd", probs, value_part, preferred_element_type=jnp.float32)
        outputs.append(mixed.astype(jnp.bfloat16).reshape(row_block, columns))
    attended = jnp.concatenate(outputs, axis=0)
    out_cols = lax.all_gather(out_weight, "seq", axis=1, tiled=True)
    rows = attended
    attn_sum = lax.psum_scatter(
        jnp.dot(rows, out_cols, preferred_element_type=jnp.float32),
        "head",
        scatter_dimension=0,
        tiled=True,
    )
    middle = (tokens.astype(jnp.float32) + attn_sum).astype(jnp.bfloat16)
    normed_two = layer_norm(middle, norm2_gain)
    up_full = lax.all_gather(up_weight, "seq", axis=0, tiled=True)
    hidden = jax.nn.gelu(
        jnp.dot(
            lax.all_gather(normed_two, "head", axis=0, tiled=True),
            up_full,
            preferred_element_type=jnp.float32,
        ),
        approximate=True,
    ).astype(jnp.bfloat16)
    down_full = lax.all_gather(down_weight, "seq", axis=1, tiled=True)
    rows = hidden
    mlp_sum = lax.psum_scatter(
        jnp.dot(rows, down_full, preferred_element_type=jnp.float32),
        "head",
        scatter_dimension=0,
        tiled=True,
    )
    return (middle.astype(jnp.float32) + mlp_sum).astype(jnp.bfloat16)


def solution(mesh):
    return jax.shard_map(
        local,
        mesh=mesh,
        in_specs=(
            P(("seq", "head"), None),
            P("seq"),
            P("seq"),
            P(),
            P("seq", None, "head"),
            P(None, "head", None),
            P("head", "seq"),
            P(),
            P("seq", "head"),
            P("head", "seq"),
        ),
        out_specs=P(("seq", "head"), None),
        check_vma=False,
    )
```

profile of v0, /device:TPU:2, one launch (start us, length us, event | category | flops | bytes accessed | tf_op | source)
XLA Modules:
  0.0 375.9 jit_solution(14275291162131240596)
XLA Ops:
  7.4 1.1 convert_reduce_fusion.1
  8.5 1.2 fusion.30
  9.7 1.9 fusion.32
  11.6 0.0 reduce-scatter.3.cloned.1.call-start
  11.6 0.7 slice_bitcast_fusion
  12.3 0.1 mul.135
  12.4 52.3 %all_gather.19 = bf16[1024,3,128]{2,0,1:T(8,128)(2,1)S(1)} all-gather(bf16[32,3,128]{2,0,1:T(8,128)(2,1)} %param.14), channel_id=1, replica_groups=mesh['seq'=32,'head'=8] {'seq'}, dimensions={0}, use_global_device_ids=true | all-gather | bytes 811008 | tf_op jit(solution)/shard_map/all_gather | solution.py:54
  64.7 0.3 copy.25
  65.0 47.4 %all_gather.20 = bf16[128,1024]{0,1:T(8,128)(2,1)S(1)} all-gather(bf16[128,32]{0,1:T(8,128)(2,1)S(1)} %copy-done.3), channel_id=1, replica_groups=mesh['seq'=32,'head'=8] {'seq'}, dimensions={1}, use_global_device_ids=true | all-gather | bytes 270336 | tf_op jit(solution)/shard_map/all_gather | solution.py:90
  112.5 1.5 compare_and_fusion
  114.0 2.9 fusion.10
  116.9 0.2 copy.26
  117.2 0.2 copy.27
  117.4 0.1 fusion.53
  117.5 0.2 copy.29
  117.7 0.1 multiply_reduce_fusion
  117.8 3.2 collective-permute-start
  121.0 2.8 collective-permute-start.1
  123.8 0.1 multiply_convert_fusion
  123.9 2.9 collective-permute-done.1
  126.8 0.1 pad_maximum_fusion.3
  126.9 0.2 copy.30
  127.1 0.2 copy.28
  127.2 0.2 copy.31
  127.4 0.2 copy.32
  127.6 1.0 fusion.1
  128.6 1.0 fusion
  129.5 0.9 fusion.14
  130.5 0.9 fusion.15
  131.4 2.7 fusion.35
  134.1 0.0 all-gather.9.cloned.1.call-start
  134.2 0.5 all-gather.9.cloned.1.call-update
  134.7 0.0 all-gather.11.cloned.1.call-start
  134.8 0.5 all-gather.11.cloned.1.call-update
  135.3 0.0 all-gather.7.cloned.1.call-start
  135.4 41.5 %reduce-scatter.3.cloned.1.call-done = f32[128,1024]{1,0:T(8,128)} async-done(((f32[1024,1024]{1,0:T(8,128)}), f32[128,1024]{1,0:T(8,128)}) %reduce-scatter.3.cloned.1.call-update) | async-done | bytes 524304 | tf_op jit(solution)/shard_map/reduce_scatter | solution.py:92
  176.9 1.2 convert_reduce_fusion
  178.1 0.2 fusion.27
  178.3 0.9 fusion.29
  179.2 0.0 all-gather.7.cloned.1.call-update
  179.2 0.0 reduce-scatter.5.cloned.1.call-start
  179.3 35.0 %all-gather.9.cloned.1.call-done = bf16[1024,512]{1,0:T(8,128)(2,1)} async-done(((bf16[32,512]{1,0:T(8,128)(2,1)}), bf16[1024,512]{1,0:T(8,128)(2,1)}) %all-gather.9.cloned.1.call-update) | async-done | bytes 1048592 | tf_op jit(solution)/shard_map/all_gather | solution.py:100
  214.3 76.5 %all-gather.11.cloned.1.call-done = bf16[512,1024]{0,1:T(8,128)(2,1)} async-done(((bf16[512,32]{0,1:T(8,128)(2,1)}), bf16[512,1024]{0,1:T(8,128)(2,1)}) %all-gather.11.cloned.1.call-update) | async-done | bytes 1048592 | tf_op jit(solution)/shard_map/all_gather | solution.py:109
  290.8 28.3 %all-gather.7.cloned.1.call-done = bf16[1024,1024]{1,0:T(8,128)(2,1)} async-done(((bf16[128,1024]{1,0:T(8,128)(2,1)}), bf16[1024,1024]{1,0:T(8,128)(2,1)}) %all-gather.7.cloned.1.call-update) | async-done | bytes 2097168 | tf_op jit(solution)/shard_map/all_gather | solution.py:103
  319.1 6.7 %fusion.16 = f32[1024,1024]{1,0:T(8,128)} fusion(bf16[512,1024]{0,1:T(8,128)(2,1)} %all-gather.11.cloned.1.call-done, bf16[1024,1024]{1,0:T(8,128)(2,1)} %all-gather.7.cloned.1.call-done, bf16[1024,512]{1,0:T(8,128)(2,1)} %all-gather.9.cloned.1.call-done), kind=kOutput, calls=%fused_computation.23 | convolution fusion | flops 2152202240 | bytes 8388608 | tf_op jit(solution)/shard_map/dot_general | solution.py:112
  325.8 0.0 reduce-scatter.5.cloned.1.call-update
  325.8 40.7 %reduce-scatter.5.cloned.1.call-done = f32[128,1024]{1,0:T(8,128)} async-done(((f32[1024,1024]{1,0:T(8,128)}), f32[128,1024]{1,0:T(8,128)}) %reduce-scatter.5.cloned.1.call-update) | async-done | bytes 524304 | tf_op jit(solution)/shard_map/reduce_scatter | solution.py:111
  366.5 1.8 fusion.34
  (33 shorter events, 0.3 us)
Async XLA Ops:
  7.4 57.7 %copy-start.3 = (bf16[128,32]{0,1:T(8,128)(2,1)S(1)}, bf16[128,32]{0,1:T(8,128)(2,1)}, u32[]{:S(2)}) copy-start(bf16[128,32]{0,1:T(8,128)(2,1)} %param.16) | copy-start | bytes 24580
  7.4 105.1 %copy-start.5 = (s32[1024]{0:T(1024)S(1)}, s32[1024]{0:T(1024)}, u32[]{:S(2)}) copy-start(s32[1024]{0:T(1024)} %param.12) | copy-start | bytes 12292
  7.4 105.1 %copy-start.6 = (s32[1024]{0:T(1024)S(1)}, s32[1024]{0:T(1024)}, u32[]{:S(2)}) copy-start(s32[1024]{0:T(1024)} %param.11) | copy-start | bytes 12292
  7.4 106.6 %all-gather.5.cloned.1.call-start = ((), (), s32[]{:S(2)}) async-start(), calls=%async_computation.2 | async-start | bytes 2359296 | tf_op jit(solution)/shard_map/all_gather | solution.py:57
  11.6 165.3 %reduce-scatter.3.cloned.1.call-start = ((), (), s32[]{:S(2)}) async-start(), calls=%async_computation.3 | async-start | bytes 4718592 | tf_op jit(solution)/shard_map/reduce_scatter | solution.py:92
  117.8 9.8 %copy-start.2 = (pred[512,640]{1,0:T(8,128)(4,1)S(1)}, pred[512,640]{1,0:T(8,128)(4,1)}, u32[]{:S(2)}) copy-start(pred[512,640]{1,0:T(8,128)(4,1)} %get-tuple-element.27) | copy-start | bytes 983044
  117.8 6.1 %collective-permute-start = (bf16[64,2,128]{2,0,1:T(8,128)(2,1)S(1)}, bf16[64,2,128]{2,0,1:T(8,128)(2,1)S(1)}, u32[]{:S(2)}, u32[]{:S(2)}) collective-permute-start(bf16[64,2,128]{2,0,1:T(8,128)(2,1)S(1)} %get-tuple-element.15), channel_id=1, source_target_pairs={{0,8},{8,16},{16,24},{24,32},{32,40},{40,48},{48,56},{56,64},{64,7... | collective-permute-start | bytes 98312 | tf_op jit(solution)/shard_map/ppermute | solution.py:17
  121.0 5.8 %collective-permute-start.1 = (bf16[64,2,128]{2,0,1:T(8,128)(2,1)S(1)}, bf16[64,2,128]{2,0,1:T(8,128)(2,1)S(1)}, u32[]{:S(2)}, u32[]{:S(2)}) collective-permute-start(bf16[64,2,128]{2,0,1:T(8,128)(2,1)S(1)} %get-tuple-element.16), channel_id=1, source_target_pairs={{8,0},{16,8},{24,16},{32,24},{40,32},{48,40},{56,48},{64,56},{72,6... | collective-permute-start | bytes 98312 | tf_op jit(solution)/shard_map/ppermute | solution.py:18
  127.4 1.2 copy-start.1
  134.1 42.8 %copy-start = (bf16[128,1024]{1,0:T(8,128)(2,1)S(1)}, bf16[128,1024]{1,0:T(8,128)(2,1)}, u32[]{:S(2)}) copy-start(bf16[128,1024]{1,0:T(8,128)(2,1)} %param.10) | copy-start | bytes 786436
  134.1 44.2 %copy-start.4 = (f32[1024]{0:T(1024)S(1)}, f32[1024]{0:T(1024)}, u32[]{:S(2)}) copy-start(f32[1024]{0:T(1024)} %param.17) | copy-start | bytes 12292
  134.1 80.2 %all-gather.9.cloned.1.call-start = ((), (), s32[]{:S(2)}) async-start(), calls=%async_computation.5 | async-start | bytes 1081344 | tf_op jit(solution)/shard_map/all_gather | solution.py:100
  134.7 156.0 %all-gather.11.cloned.1.call-start = ((), (), s32[]{:S(2)}) async-start(), calls=%async_computation.6 | async-start | bytes 1081344 | tf_op jit(solution)/shard_map/all_gather | solution.py:109
  135.3 183.7 %all-gather.7.cloned.1.call-start = ((), (), s32[]{:S(2)}) async-start(), calls=%async_computation.4 | async-start | bytes 2359296 | tf_op jit(solution)/shard_map/all_gather | solution.py:103
  179.2 187.2 %reduce-scatter.5.cloned.1.call-start = ((), (), s32[]{:S(2)}) async-start(), calls=%async_computation.7 | async-start | bytes 4718592 | tf_op jit(solution)/shard_map/reduce_scatter | solution.py:111
Sparse Core Ops, SparseCore 0:
  11.7 30.6 all-gather.4
  134.3 42.5 reduce-scatter.2
Sparse Core Ops, SparseCore 1:
  137.2 77.1 all-gather.8
  216.8 73.9 all-gather.10
  292.5 26.5 all-gather.6
  325.9 40.6 reduce-scatter.4
where the time goes:
time: 376 us
  waiting for transfers between devices  226 us (60%)
  blocking collectives  99.7 us (27%)
  matrix products  16.1 us (4%)
  between operations  15.3 us (4%)
  other arithmetic  10.2 us (3%)
  starting transfers between devices  6.18 us (2%)
    all_gather x1, waiting for transfers between devices, local(): down_full = lax.all_gather(down_weight, 'seq', axis=1, tiled=True)  76.5 us
    all_gather x1, blocking collectives, local(): lax.all_gather(qkv_weight, 'seq', axis=0, tiled=True)  52.3 us
    all_gather x1, blocking collectives, local(): out_cols = lax.all_gather(out_weight, 'seq', axis=1, tiled=True)  47.4 us
    reduce_scatter x1, waiting for transfers between devices, local(): lax.psum_scatter(jnp.dot(rows, out_cols, preferred_element_type=jnp.float...  41.5 us
    reduce_scatter x1, waiting for transfers between devices, local(): lax.psum_scatter(jnp.dot(rows, down_full, preferred_element_type=jnp.floa...  40.7 us
    all_gather x1, waiting for transfers between devices, local(): up_full = lax.all_gather(up_weight, 'seq', axis=0, tiled=True)  35 us
    all_gather x1, waiting for transfers between devices, local(): lax.all_gather(normed_two, 'head', axis=0, tiled=True)  28.3 us
  transfers between devices with their start and end apart: 8, of which 6 were waited for; matrix products, arithmetic and copies ran while one was open for 1% of the time, Pallas kernels for 0%

commit v1 on v0

--- a/solution.py
+++ b/solution.py
@@ -5,6 +5,19 @@
 from jax.sharding import PartitionSpec as P
 
 WIN_MOST = 64
+
+
+def ring_gather(x, axis, dim):
+    ways = lax.axis_size(axis)
+    up = [(d, (d + 1) % ways) for d in range(ways)]
+    down = [(d, (d - 1) % ways) for d in range(ways)]
+    earlier, later = ([x], [x])
+    for _ in range(ways // 2):
+        earlier.append(lax.ppermute(earlier[-1], axis, up))
+    for _ in range((ways - 1) // 2):
+        later.append(lax.ppermute(later[-1], axis, down))
+    line = jnp.concatenate([*earlier[::-1], *later[1:]], axis=dim)
+    return jnp.roll(line, (lax.axis_index(axis) - ways // 2) * x.shape[dim], axis=dim)
 
 
 def extended(value, sides, width):
@@ -99,11 +112,7 @@
     normed_two = layer_norm(middle, norm2_gain)
     up_full = lax.all_gather(up_weight, "seq", axis=0, tiled=True)
     hidden = jax.nn.gelu(
-        jnp.dot(
-            lax.all_gather(normed_two, "head", axis=0, tiled=True),
-            up_full,
-            preferred_element_type=jnp.float32,
-        ),
+        jnp.dot(ring_gather(normed_two, "head", 0), up_full, preferred_element_type=jnp.float32),
         approximate=True,
     ).astype(jnp.bfloat16)
     down_full = lax.all_gather(down_weight, "seq", axis=1, tiled=True)

time: 376 us -> 345 us (0.918)
  waiting for transfers between devices: 226 us -> 176 us
  local copies, waits for them, and re-layouts: 2.4 us -> 11.8 us
  starting transfers between devices: 6.18 us -> 15.3 us
    all_gather x1, waiting for transfers between devices: 35 us -> 0.01 us  [local(): up_full = lax.all_gather(up_weight, 'seq', axis=0, tiled=True)]
    all_gather x1 -> x0, waiting for transfers between devices: 28.3 us -> none  [local(): lax.all_gather(normed_two, 'head', axis=0, tiled=True)]
    ppermute x0 -> x7, waiting for transfers between devices: none -> 18.8 us  [the longest x4 18.8 us: ring_gather(): earlier.append(lax.ppermute(earlier[-1], axis, up))]
    unnamed x14 -> x29, local copies, waits for them, and re-layouts: 0.03 us -> 9.4 us
    ppermute x0 -> x7, starting transfers between devices: none -> 8.9 us  [the longest x3 8.87 us: ring_gather(): later.append(lax.ppermute(later[-1], axis, down))]
    all_gather x1, waiting for transfers between devices: 76.5 us -> 72.2 us  [local(): down_full = lax.all_gather(down_weight, 'seq', axis=1, tiled=True)]
  transfers between devices with their start and end apart: 8 -> 14, of which waited for: 6 -> 8; matrix products, arithmetic and copies ran while one was open for 1% -> 5% of each run, Pallas kernels for 0% -> 0%
where the time goes in v1:
time: 345 us
  waiting for transfers between devices  176 us (51%)
  blocking collectives  99.7 us (29%)
  matrix products  16.1 us (5%)
  starting transfers between devices  15.3 us (4%)
  between operations  14.9 us (4%)
  local copies, waits for them, and re-layouts  11.8 us (3%)
  other arithmetic  11.3 us (3%)
    all_gather x1, waiting for transfers between devices, local(): down_full = lax.all_gather(down_weight, 'seq', axis=1, tiled=True)  72.2 us
    all_gather x1, blocking collectives, local(): lax.all_gather(qkv_weight, 'seq', axis=0, tiled=True)  52.5 us
    all_gather x1, blocking collectives, local(): out_cols = lax.all_gather(out_weight, 'seq', axis=1, tiled=True)  47.2 us
    reduce_scatter x1, waiting for transfers between devices, local(): lax.psum_scatter(jnp.dot(rows, out_cols, preferred_element_type=jnp.float...  42.1 us
    reduce_scatter x1, waiting for transfers between devices, local(): lax.psum_scatter(jnp.dot(rows, down_full, preferred_element_type=jnp.floa...  39.2 us
    ppermute x4, waiting for transfers between devices, ring_gather(): earlier.append(lax.ppermute(earlier[-1], axis, up))  18.8 us
    unnamed x29, local copies, waits for them, and re-layouts  9.4 us
    ppermute x3, starting transfers between devices, ring_gather(): later.append(lax.ppermute(later[-1], axis, down))  8.87 us
  transfers between devices with their start and end apart: 14, of which 8 were waited for; matrix products, arithmetic and copies ran while one was open for 5% of the time, Pallas kernels for 0%

profile of v1, /device:TPU:2, one launch (start us, length us, event | category | flops | bytes accessed | tf_op | source)
XLA Modules:
  0.0 344.7 jit_solution(7696315915873699701)
XLA Ops:
  7.4 1.1 convert_reduce_fusion.1
  8.5 1.2 fusion.31
  9.7 1.9 fusion.33
  11.6 52.5 %all_gather.16 = bf16[1024,3,128]{2,0,1:T(8,128)(2,1)S(1)} all-gather(bf16[32,3,128]{2,0,1:T(8,128)(2,1)} %param.14), channel_id=1, replica_groups=mesh['seq'=32,'head'=8] {'seq'}, dimensions={0}, use_global_device_ids=true | all-gather | bytes 811008 | tf_op jit(solution)/shard_map/all_gather | solution.py:67
  64.1 0.3 copy.25
  64.5 47.2 %all_gather.17 = bf16[128,1024]{0,1:T(8,128)(2,1)S(1)} all-gather(bf16[128,32]{0,1:T(8,128)(2,1)S(1)} %copy-done.4), channel_id=1, replica_groups=mesh['seq'=32,'head'=8] {'seq'}, dimensions={1}, use_global_device_ids=true | all-gather | bytes 270336 | tf_op jit(solution)/shard_map/all_gather | solution.py:103
  111.8 1.4 compare_and_fusion
  113.2 2.9 fusion.10
  116.8 3.2 collective-permute-start
  120.0 2.7 collective-permute-start.1
  123.2 2.7 collective-permute-done.1
  126.6 1.0 fusion
  127.6 1.0 fusion.1
  128.5 0.9 fusion.19
  129.5 0.9 fusion.18
  130.4 2.7 fusion.36
  133.2 0.5 all-gather.6.cloned.1.call-update
  133.8 42.1 %reduce-scatter.3.cloned.1.call-done = f32[128,1024]{1,0:T(8,128)} async-done(((f32[1024,1024]{1,0:T(8,128)}), f32[128,1024]{1,0:T(8,128)}) %reduce-scatter.3.cloned.1.call-update) | async-done | bytes 524304 | tf_op jit(solution)/shard_map/reduce_scatter | solution.py:105
  175.9 1.2 convert_reduce_fusion
  177.3 0.2 fusion.30
  177.6 7.0 %collective-permute-done.2 = bf16[128,1024]{1,0:T(8,128)(2,1)S(1)} collective-permute-done((bf16[128,1024]{1,0:T(8,128)(2,1)S(1)}, bf16[128,1024]{1,0:T(8,128)(2,1)S(1)}, u32[]{:S(2)}, u32[]{:S(2)}) %collective-permute-start.2) | collective-permute-done | bytes 262176 | tf_op jit(solution)/shard_map/ppermute | solution.py:16
  184.6 3.0 collective-permute-start.6
  187.5 4.1 %collective-permute-done.3 = bf16[128,1024]{1,0:T(8,128)(2,1)S(1)} collective-permute-done((bf16[128,1024]{1,0:T(8,128)(2,1)S(1)}, bf16[128,1024]{1,0:T(8,128)(2,1)S(1)}, u32[]{:S(2)}, u32[]{:S(2)}) %collective-permute-start.3) | collective-permute-done | bytes 262176 | tf_op jit(solution)/shard_map/ppermute | solution.py:16
  191.6 3.0 collective-permute-start.7
  194.5 4.0 %collective-permute-done.4 = bf16[128,1024]{1,0:T(8,128)(2,1)S(1)} collective-permute-done((bf16[128,1024]{1,0:T(8,128)(2,1)S(1)}, bf16[128,1024]{1,0:T(8,128)(2,1)S(1)}, u32[]{:S(2)}, u32[]{:S(2)}) %collective-permute-start.4) | collective-permute-done | bytes 262176 | tf_op jit(solution)/shard_map/ppermute | solution.py:16
  198.6 0.2 reduce-scatter.5.cloned.1.call-start
  198.9 3.0 collective-permute-start.8
  201.9 3.7 %collective-permute-done.5 = bf16[128,1024]{1,0:T(8,128)(2,1)S(1)} collective-permute-done((bf16[128,1024]{1,0:T(8,128)(2,1)S(1)}, bf16[128,1024]{1,0:T(8,128)(2,1)S(1)}, u32[]{:S(2)}, u32[]{:S(2)}) %collective-permute-start.5) | collective-permute-done | bytes 262176 | tf_op jit(solution)/shard_map/ppermute | solution.py:16
  205.6 0.7 constant_dynamic-update-slice_fusion.15
  206.3 0.7 constant_dynamic-update-slice_fusion.14
  207.1 0.7 constant_dynamic-update-slice_fusion.13
  207.8 0.7 constant_dynamic-update-slice_fusion.12
  208.5 0.9 constant_dynamic-update-slice_fusion.11
  209.4 0.7 constant_dynamic-update-slice_fusion.10
  210.2 0.7 constant_dynamic-update-slice_fusion.9
  210.9 0.7 constant_dynamic-update-slice_fusion.8
  211.6 0.7 constant_dynamic-update-slice_fusion.7
  212.3 0.7 constant_dynamic-update-slice_fusion.6
  213.0 0.7 constant_dynamic-update-slice_fusion.5
  213.8 0.7 constant_dynamic-update-slice_fusion.4
  214.5 0.9 constant_dynamic-update-slice_fusion.3
  215.4 0.7 constant_dynamic-update-slice_fusion.2
  216.1 0.7 constant_dynamic-update-slice_fusion.1
  216.8 0.8 constant_dynamic-update-slice_fusion
  217.6 72.2 %all-gather.8.cloned.1.call-done = bf16[512,1024]{0,1:T(8,128)(2,1)} async-done(((bf16[512,32]{0,1:T(8,128)(2,1)}), bf16[512,1024]{0,1:T(8,128)(2,1)}) %all-gather.8.cloned.1.call-update) | async-done | bytes 1048592 | tf_op jit(solution)/shard_map/all_gather | solution.py:118
  289.8 6.7 %fusion.21 = f32[1024,1024]{1,0:T(8,128)} fusion(bf16[512,1024]{0,1:T(8,128)(2,1)} %all-gather.8.cloned.1.call-done, bf16[1024,512]{1,0:T(8,128)(2,1)} %all-gather.6.cloned.1.call-done, bf16[2048,1024]{1,0:T(8,128)(2,1)} %constant_dynamic-update-slice_fusion, s32[]{:T(128)S(6)} %select_n.23), kind=kOutput, calls=%fused_computation.25 | convolution fusion | flops 2152202240 | bytes 8388612 | tf_op jit(solution)/shard_map/dot_general | solution.py:121
  296.5 39.2 %reduce-scatter.5.cloned.1.call-done = f32[128,1024]{1,0:T(8,128)} async-done(((f32[1024,1024]{1,0:T(8,128)}), f32[128,1024]{1,0:T(8,128)}) %reduce-scatter.5.cloned.1.call-update) | async-done | bytes 524304 | tf_op jit(solution)/shard_map/reduce_scatter | solution.py:120
  335.7 1.8 fusion.35
  (62 shorter events, 2.4 us)
Async XLA Ops:
  7.4 57.0 %copy-start.7 = (f32[2,2,64]{2,1,0:T(2,128)S(1)}, f32[2,2,64]{2,1,0:T(2,128)}, u32[]{:S(2)}) copy-start(f32[2,2,64]{2,1,0:T(2,128)} %param.15) | copy-start | bytes 3076
  7.4 57.1 %copy-start.4 = (bf16[128,32]{0,1:T(8,128)(2,1)S(1)}, bf16[128,32]{0,1:T(8,128)(2,1)}, u32[]{:S(2)}) copy-start(bf16[128,32]{0,1:T(8,128)(2,1)} %param.16) | copy-start | bytes 24580
  7.4 104.4 %copy-start.6 = (s32[1024]{0:T(1024)S(1)}, s32[1024]{0:T(1024)}, u32[]{:S(2)}) copy-start(s32[1024]{0:T(1024)} %param.11) | copy-start | bytes 12292
  7.4 104.4 %copy-start.5 = (s32[1024]{0:T(1024)S(1)}, s32[1024]{0:T(1024)}, u32[]{:S(2)}) copy-start(s32[1024]{0:T(1024)} %param.12) | copy-start | bytes 12292
  7.4 105.8 %all-gather.4.cloned.1.call-start = ((), (), s32[]{:S(2)}) async-start(), calls=%async_computation.2 | async-start | bytes 2359296 | tf_op jit(solution)/shard_map/all_gather | solution.py:70
  11.6 164.3 %reduce-scatter.3.cloned.1.call-start = ((), (), s32[]{:S(2)}) async-start(), calls=%async_computation.3 | async-start | bytes 4718592 | tf_op jit(solution)/shard_map/reduce_scatter | solution.py:105
  116.8 9.8 %copy-start.2 = (pred[512,640]{1,0:T(8,128)(4,1)S(1)}, pred[512,640]{1,0:T(8,128)(4,1)}, u32[]{:S(2)}) copy-start(pred[512,640]{1,0:T(8,128)(4,1)} %get-tuple-element.28) | copy-start | bytes 983044
  116.8 6.4 %collective-permute-start = (bf16[64,2,128]{2,0,1:T(8,128)(2,1)S(1)}, bf16[64,2,128]{2,0,1:T(8,128)(2,1)S(1)}, u32[]{:S(2)}, u32[]{:S(2)}) collective-permute-start(bf16[64,2,128]{2,0,1:T(8,128)(2,1)S(1)} %get-tuple-element.15), channel_id=1, source_target_pairs={{0,8},{8,16},{16,24},{24,32},{32,40},{40,48},{48,56},{56,64},{64,7... | collective-permute-start | bytes 98312 | tf_op jit(solution)/shard_map/ppermute | solution.py:30
  120.0 5.8 %collective-permute-start.1 = (bf16[64,2,128]{2,0,1:T(8,128)(2,1)S(1)}, bf16[64,2,128]{2,0,1:T(8,128)(2,1)S(1)}, u32[]{:S(2)}, u32[]{:S(2)}) collective-permute-start(bf16[64,2,128]{2,0,1:T(8,128)(2,1)S(1)} %get-tuple-element.16), channel_id=1, source_target_pairs={{8,0},{16,8},{24,16},{32,24},{40,32},{48,40},{56,48},{64,56},{72,6... | collective-permute-start | bytes 98312 | tf_op jit(solution)/shard_map/ppermute | solution.py:31
  125.9 1.7 copy-start.1
  133.1 42.8 %copy-start = (bf16[128,1024]{1,0:T(8,128)(2,1)S(1)}, bf16[128,1024]{1,0:T(8,128)(2,1)}, u32[]{:S(2)}) copy-start(bf16[128,1024]{1,0:T(8,128)(2,1)} %param.10) | copy-start | bytes 786436
  133.1 44.2 %copy-start.3 = (f32[1024]{0:T(1024)S(1)}, f32[1024]{0:T(1024)}, u32[]{:S(2)}) copy-start(f32[1024]{0:T(1024)} %param.17) | copy-start | bytes 12292
  133.1 84.4 %all-gather.6.cloned.1.call-start = ((), (), s32[]{:S(2)}) async-start(), calls=%async_computation.4 | async-start | bytes 1081344 | tf_op jit(solution)/shard_map/all_gather | solution.py:113
  133.7 156.0 %all-gather.8.cloned.1.call-start = ((), (), s32[]{:S(2)}) async-start(), calls=%async_computation.5 | async-start | bytes 1081344 | tf_op jit(solution)/shard_map/all_gather | solution.py:118
  177.6 7.0 %collective-permute-start.2 = (bf16[128,1024]{1,0:T(8,128)(2,1)S(1)}, bf16[128,1024]{1,0:T(8,128)(2,1)S(1)}, u32[]{:S(2)}, u32[]{:S(2)}) collective-permute-start(bf16[128,1024]{1,0:T(8,128)(2,1)S(1)} %fusion.30), channel_id=1, source_target_pairs={{0,1},{1,2},{2,3},{3,4},{4,5},{5,6},{6,7},{7,0},{8,9},{9,10},{10,1... | collective-permute-start | bytes 786440 | tf_op jit(solution)/shard_map/ppermute | solution.py:16
  184.6 7.0 %collective-permute-start.3 = (bf16[128,1024]{1,0:T(8,128)(2,1)S(1)}, bf16[128,1024]{1,0:T(8,128)(2,1)S(1)}, u32[]{:S(2)}, u32[]{:S(2)}) collective-permute-start(bf16[128,1024]{1,0:T(8,128)(2,1)S(1)} %collective-permute-done.2), channel_id=1, source_target_pairs={{0,1},{1,2},{2,3},{3,4},{4,5},{5,6},{6,7},{7,0},{8,9},{9,10},{10,1... | collective-permute-start | bytes 786440 | tf_op jit(solution)/shard_map/ppermute | solution.py:16
  184.6 7.0 %collective-permute-start.6 = (bf16[128,1024]{1,0:T(8,128)(2,1)S(1)}, bf16[128,1024]{1,0:T(8,128)(2,1)S(1)}, u32[]{:S(2)}, u32[]{:S(2)}) collective-permute-start(bf16[128,1024]{1,0:T(8,128)(2,1)S(1)} %fusion.30), channel_id=1, source_target_pairs={{0,7},{1,0},{2,1},{3,2},{4,3},{5,4},{6,5},{7,6},{8,15},{9,8},{10,9... | collective-permute-start | bytes 786440 | tf_op jit(solution)/shard_map/ppermute | solution.py:18
  191.6 7.0 %collective-permute-start.4 = (bf16[128,1024]{1,0:T(8,128)(2,1)S(1)}, bf16[128,1024]{1,0:T(8,128)(2,1)S(1)}, u32[]{:S(2)}, u32[]{:S(2)}) collective-permute-start(bf16[128,1024]{1,0:T(8,128)(2,1)S(1)} %collective-permute-done.3), channel_id=1, source_target_pairs={{0,1},{1,2},{2,3},{3,4},{4,5},{5,6},{6,7},{7,0},{8,9},{9,10},{10,1... | collective-permute-start | bytes 786440 | tf_op jit(solution)/shard_map/ppermute | solution.py:16
  191.6 7.3 %collective-permute-start.7 = (bf16[128,1024]{1,0:T(8,128)(2,1)S(1)}, bf16[128,1024]{1,0:T(8,128)(2,1)S(1)}, u32[]{:S(2)}, u32[]{:S(2)}) collective-permute-start(bf16[128,1024]{1,0:T(8,128)(2,1)S(1)} %collective-permute-done.6), channel_id=1, source_target_pairs={{0,7},{1,0},{2,1},{3,2},{4,3},{5,4},{6,5},{7,6},{8,15},{9,8},{10,9... | collective-permute-start | bytes 786440 | tf_op jit(solution)/shard_map/ppermute | solution.py:18
  198.6 7.0 %collective-permute-start.5 = (bf16[128,1024]{1,0:T(8,128)(2,1)S(1)}, bf16[128,1024]{1,0:T(8,128)(2,1)S(1)}, u32[]{:S(2)}, u32[]{:S(2)}) collective-permute-start(bf16[128,1024]{1,0:T(8,128)(2,1)S(1)} %collective-permute-done.4), channel_id=1, source_target_pairs={{0,1},{1,2},{2,3},{3,4},{4,5},{5,6},{6,7},{7,0},{8,9},{9,10},{10,1... | collective-permute-start | bytes 786440 | tf_op jit(solution)/shard_map/ppermute | solution.py:16
  198.6 137.1 %reduce-scatter.5.cloned.1.call-start = ((), (), s32[]{:S(2)}) async-start(), calls=%async_computation.6 | async-start | bytes 4718592 | tf_op jit(solution)/shard_map/reduce_scatter | solution.py:120
  198.9 12.0 %collective-permute-start.8 = (bf16[128,1024]{1,0:T(8,128)(2,1)S(1)}, bf16[128,1024]{1,0:T(8,128)(2,1)S(1)}, u32[]{:S(2)}, u32[]{:S(2)}) collective-permute-start(bf16[128,1024]{1,0:T(8,128)(2,1)S(1)} %collective-permute-done.7), channel_id=1, source_target_pairs={{0,7},{1,0},{2,1},{3,2},{4,3},{5,4},{6,5},{7,6},{8,15},{9,8},{10,9... | collective-permute-start | bytes 786440 | tf_op jit(solution)/shard_map/ppermute | solution.py:18
Sparse Core Ops, SparseCore 0:
  11.7 30.6 all-gather.3
  133.3 42.5 reduce-scatter.2
  296.6 39.0 reduce-scatter.4
Sparse Core Ops, SparseCore 1:
  136.2 77.1 all-gather.5
  215.8 73.9 all-gather.7
